TPU v7x, 32 devices: a whole 2x2x4 slice. The times are simulated.
32 devices in a mesh: groups: 2 (over y), train: 4 (over z), query: 2 (over x), feat: 2 (over core).
Axes of the slice: x: 2, y: 2, z: 4, core: 2. Of those that a mesh axis runs over, the one named last changes fastest.
Arguments:
- train_pool: float32 [320, 8192], P(('groups', 'train'), 'feat'), parts along dimension 0, may hold values from -130 to 130
- query_pool: float32 [864, 8192], P(('groups', 'query'), 'feat'), parts along dimension 0, may hold values from -16640 to 16640
- train_pick: int32 [256], P(('groups', 'train')), parts along dimension 0, may hold values from 0 to 159, as said below
- query_pick: int32 [768], P(('groups', 'query')), parts along dimension 0, may hold values from 0 to 431, as said below
Outputs:
- scores: float32 [768, 128], P(('groups', 'query'), 'train'), parts along dimension 0
There are 2 independent parts, one for each index of `groups`. A program takes and returns all parts, laid end to end along the dimension named above; each array names one. Nothing has to cross between parts.
Inputs may be any that keep to these rules, and one draw needn't show every extreme that they name: `train_pick`: the entries for training block t (positions t * 32 to (t + 1) * 32 - 1) are distinct and lie in t * 40 to (t + 1) * 40 - 1. `query_pick`: the entries for query block q (positions q * 192 to (q + 1) * 192 - 1) are distinct and lie in q * 216 to (q + 1) * 216 - 1.
All inputs are finite; a program needn't handle non-finite values.
Results may differ from a plain program's by a relative error of at most 0.0003.
Values sent between devices are 32-bit elements; how exact they have to be, the bound alone decides.
A program may use at most 64 MiB of HBM per device.

v0:
```python
import jax
import jax.numpy as jnp
from jax import lax
from jax.sharding import PartitionSpec as P

WIDTH = 8192


def on_device(train_pool, query_pool, train_pick, query_pick):
    highest = lax.Precision.HIGHEST
    block_rows = train_pick.shape[0]
    train_index = lax.axis_index("train")
    query_index = lax.axis_index("query")
    train_rows = jnp.take(train_pool, train_pick - train_index * train_pool.shape[0], axis=0)
    query_rows = jnp.take(query_pool, query_pick - query_index * query_pool.shape[0], axis=0)
    cross_tile = jnp.dot(
        query_rows, train_rows.T, precision=highest, preferred_element_type=jnp.float32
    )
    kernel_part = jnp.dot(
        train_rows,
        lax.all_gather(train_rows, "train", axis=0, tiled=True).T,
        precision=highest,
        preferred_element_type=jnp.float32,
    )
    cross_tile, kernel_part = lax.psum((cross_tile, kernel_part), "feat")
    kernel = lax.all_gather(kernel_part, "train", axis=0, tiled=True)
    order_size = kernel.shape[0]
    row_iota = lax.broadcasted_iota(jnp.int32, (order_size, order_size), 0)
    col_iota = lax.broadcasted_iota(jnp.int32, (order_size, order_size), 1)
    identity = (row_iota == col_iota).astype(jnp.float32)
    factor = jnp.linalg.cholesky(kernel + 0.5 * WIDTH * identity)
    sel_rows = lax.broadcasted_iota(jnp.int32, (order_size, block_rows), 0)
    sel_cols = (
        lax.broadcasted_iota(jnp.int32, (order_size, block_rows), 1) + train_index * block_rows
    )
    selector = (sel_rows == sel_cols).astype(jnp.float32)
    halfway = lax.linalg.triangular_solve(factor, selector, left_side=True, lower=True)
    inverse_cols = lax.linalg.triangular_solve(
        factor, halfway, left_side=True, lower=True, transpose_a=True
    )
    return jnp.dot(
        lax.all_gather(cross_tile, "train", axis=1, tiled=True),
        inverse_cols,
        precision=highest,
        preferred_element_type=jnp.float32,
    )


def solution(mesh):
    return jax.shard_map(
        on_device,
        mesh=mesh,
        in_specs=(
            P(("groups", "train"), "feat"),
            P(("groups", "query"), "feat"),
            P(("groups", "train")),
            P(("groups", "query")),
        ),
        out_specs=P(("groups", "query"), "train"),
        check_vma=False,
    )
```

profile of v0, /device:TPU:0, one launch (start us, length us, event | category | flops | bytes accessed | tf_op | source)
XLA Modules:
  0.0 140.8 jit_solution(12311087200564672442)
XLA Ops:
  6.5 0.8 compare_and_fusion
  7.4 3.0 %gather_fusion.1 = f32[32,4096]{1,0:T(8,128)} fusion(f32[40,4096]{1,0:T(8,128)} %param.4, s32[1024]{0:T(1024)S(1)} %pad_clamp_fusion), kind=kCustom, calls=%fused_computation.1 | custom fusion | bytes 1048704 | tf_op jit(solution)/shard_map/jit(_take)/gather | solution.py:14
  10.4 1.9 %broadcast_select_fusion = f32[32,4096]{1,0:T(8,128)} fusion(f32[32,4096]{1,0:T(8,128)} %gather_fusion.1, pred[32]{0:T(512)(128)(4,1)S(1)} %get-tuple-element.9), kind=kLoop, calls=%fused_computation.6 | loop fusion | flops 131072 | bytes 1048608 | tf_op jit(solution)/shard_map/jit(_take)/select_n | solution.py:14
  12.3 0.0 all-gather.2.cloned.1.call-update
  12.4 3.2 %gather_fusion = f32[192,4096]{1,0:T(8,128)} fusion(f32[216,4096]{1,0:T(8,128)S(1)} %copy-done, s32[1024]{0:T(1024)S(1)} %pad_clamp_fusion.1), kind=kCustom, calls=%fused_computation | custom fusion | bytes 6292224 | tf_op jit(solution)/shard_map/jit(_take)/gather | solution.py:15
  15.6 0.5 iota_add_fusion
  16.1 5.5 %fusion = f32[192,32]{0,1:T(8,128)} fusion(f32[32,4096]{1,0:T(8,128)} %broadcast_select_fusion, f32[192,4096]{1,0:T(8,128)} %gather_fusion, pred[192]{0:T(512)(128)(4,1)S(1)} %get-tuple-element.7), kind=kOutput, calls=%fused_computation.2 | convolution fusion | flops 302776320 | bytes 3694784 | tf_op jit(solution)/shard_map/dot_general | solution.py:16
  21.6 39.5 %all-gather.2.cloned.1.call-done = f32[128,4096]{1,0:T(8,128)} async-done(((f32[32,4096]{1,0:T(8,128)}), f32[128,4096]{1,0:T(8,128)}) %all-gather.2.cloned.1.call-update) | async-done | bytes 2097168 | tf_op jit(solution)/shard_map/all_gather | solution.py:21
  61.1 3.9 %fusion.12 = f32[32,128]{1,0:T(8,128)S(1)} fusion(f32[32,4096]{1,0:T(8,128)} %broadcast_select_fusion, f32[128,4096]{1,0:T(8,128)} %all-gather.2.cloned.1.call-done), kind=kOutput, calls=%fused_computation.30 | convolution fusion | flops 201326592 | bytes 2637824 | tf_op jit(solution)/shard_map/dot_general | solution.py:19
  65.0 4.7 %all-reduce = (f32[192,32]{0,1:T(8,128)}, f32[32,128]{1,0:T(8,128)}) all-reduce(f32[192,32]{0,1:T(8,128)} %fusion, f32[32,128]{1,0:T(8,128)S(1)} %fusion.12), channel_id=1, replica_groups=mesh['groups'=2,'train'=4,'query'=2,'feat'=2] {'feat'}, use_global_device_ids=true, to_apply=%region_0.1 | all-reduce | flops 10240 | bytes 81920 | tf_op jit(solution)/shard_map/psum | solution.py:25
  69.7 14.3 %all_gather.9 = f32[192,128]{0,1:T(8,128)} all-gather(f32[192,32]{0,1:T(8,128)} %get-tuple-element.5), channel_id=1, replica_groups=mesh['groups'=2,'train'=4,'query'=2,'feat'=2] {'train'}, dimensions={1}, use_global_device_ids=true | all-gather | bytes 122880 | tf_op jit(solution)/shard_map/all_gather | solution.py:42
  84.0 13.5 %all_gather.11 = f32[128,128]{1,0:T(8,128)S(1)} all-gather(f32[32,128]{1,0:T(8,128)} %get-tuple-element.6), channel_id=1, replica_groups=mesh['groups'=2,'train'=4,'query'=2,'feat'=2] {'train'}, dimensions={0}, use_global_device_ids=true | all-gather | bytes 81920 | tf_op jit(solution)/shard_map/all_gather | solution.py:26
  97.5 0.6 copy-done.1
  98.2 0.6 select_add_fusion
  98.8 1.6 %copy.6 = f32[128,128]{0,1:T(8,128)} copy(f32[128,128]{1,0:T(8,128)} %select_add_fusion) | data formatting | bytes 131072 | tf_op jit(solution)/shard_map/add | solution.py:31
  100.4 1.5 %fusion.9 = f32[128,128]{1,0:T(8,128)} fusion(f32[128,128]{0,1:T(8,128)} %copy.6, f32[128,128]{1,0:T(8,128)} %copy-done.1), kind=kLoop, calls=%fused_computation.14 | loop fusion | flops 81920 | bytes 196608 | tf_op jit(solution)/shard_map/jit(cholesky)/div | solution.py:31
  101.9 13.2 %cholesky.16 = f32[128,128]{1,0:T(8,128)} custom-call(f32[128,128]{1,0:T(8,128)} %fusion.9), custom_call_target="Cholesky" | custom-call | tf_op jit(solution)/shard_map/jit(cholesky)/cholesky | solution.py:31
  115.1 0.9 select_reduce_fusion
  115.9 0.6 compare_reduce_fusion
  116.6 2.1 %fusion.4 = f32[1,128,128]{2,1,0:T(8,128)} fusion(f32[128,128]{1,0:T(8,128)} %cholesky.16, pred[]{:T(512)} %compare_reduce_fusion), kind=kLoop, calls=%fused_computation.8 | loop fusion | flops 65536 | bytes 131073 | tf_op jit(solution)/shard_map/triangular_solve | solution.py:38
  118.7 11.3 %custom-call.8 = f32[1,128,128]{1,2,0:T(8,128)} custom-call(f32[1,128,128]{2,1,0:T(8,128)} %fusion.4), custom_call_target="InvertDiagBlocksLowerTriangular" | custom-call | tf_op jit(solution)/shard_map/triangular_solve | solution.py:38
  130.0 1.1 fusion.7
  131.1 1.0 fusion.5
  132.1 1.8 %fusion.13 = f32[192,32]{0,1:T(8,128)} fusion(f32[192,128]{0,1:T(8,128)} %all_gather.9, f32[128,32]{1,0:T(8,128)S(1)} %fusion.5), kind=kOutput, calls=%fused_computation.31 | convolution fusion | flops 9437184 | bytes 139264 | tf_op jit(solution)/shard_map/dot_general | solution.py:41
  (9 shorter events, 0.0 us)
Async XLA Ops:
  6.5 5.9 %copy-start = (f32[216,4096]{1,0:T(8,128)S(1)}, f32[216,4096]{1,0:T(8,128)}, u32[]{:S(2)}) copy-start(f32[216,4096]{1,0:T(8,128)} %param.5) | copy-start | bytes 10616836
  6.5 54.6 %all-gather.2.cloned.1.call-start = ((), (), s32[]{:S(2)}) async-start(), calls=%async_computation | async-start | bytes 2621440 | tf_op jit(solution)/shard_map/all_gather | solution.py:21
  7.4 5.0 %copy-start.2 = (s32[192]{0:T(256)S(1)}, s32[192]{0:T(256)}, u32[]{:S(2)}) copy-start(s32[192]{0:T(256)} %param.7) | copy-start | bytes 2308
  97.5 0.6 copy-start.1
Sparse Core Ops, SparseCore 0:
  12.5 48.6 all-gather.1
where the time goes:
time: 142 us; the launch traced here: 141 us
  waiting for transfers between devices  39.5 us (28%)
  other arithmetic  33.6 us (24%)
  blocking collectives  32.5 us (23%)
  between operations  13.5 us (10%)
  matrix products  13.3 us (9%)
  local copies, waits for them, and re-layouts  8.43 us (6%)
    all_gather x1, waiting for transfers between devices, on_device(): lax.all_gather(train_rows, 'train', axis=0, tiled=True)  39.5 us
    another operation x3, other arithmetic, on_device(): factor = jnp.linalg.cholesky(kernel + 0.5 * WIDTH * identity)  14.7 us
    all_gather x1, blocking collectives, on_device(): lax.all_gather(cross_tile, 'train', axis=1, tiled=True)  14.3 us
    all_gather x1, blocking collectives, on_device(): kernel = lax.all_gather(kernel_part, 'train', axis=0, tiled=True)  13.5 us
    another operation x2, other arithmetic, on_device(): lax.linalg.triangular_solve(factor, halfway, left_side=True, lower=True,...  13.4 us
    dot_general x1, matrix products, on_device(): jnp.dot(query_rows, train_rows.T, precision=highest, preferred_element_ty...  5.51 us
    psum x1, blocking collectives, on_device(): cross_tile, kernel_part = lax.psum((cross_tile, kernel_part), 'feat')  4.68 us
    dot_general x1, matrix products, on_device(): jnp.dot(train_rows, lax.all_gather(train_rows, 'train', axis=0, tiled=Tru...  3.89 us
  transfers between devices with their start and end apart: 1, of which 1 were waited for; matrix products, arithmetic and copies ran while one was open for 7% of the time, Pallas kernels for 0%

commit v1 on v0

v1 whole, which is shorter than its diff:
```python
import functools

import jax
import jax.numpy as jnp
from jax import lax
from jax.experimental import pallas as pl
from jax.experimental.pallas import tpu as pltpu
from jax.sharding import PartitionSpec as P

WIDTH = 8192
HIGHEST = lax.Precision.HIGHEST
NT = (((1,), (1,)), ((), ()))
CHUNKS = 4


def dot_nt(a, b):
    return lax.dot_general(a, b, NT, precision=HIGHEST, preferred_element_type=jnp.float32)


def products(n_train, n_query, n_feat, train_pick, query_pick, train_pool, query_pool,
             kernel_out, cross_out,
             train_buf, query_buf, rows, blocks, part, terms, slab, full, mine, other, tile, crosses,
             local_sem, a2a_send, a2a_recv, rs_send, rs_recv, ag_send, ag_recv,
             pair_send, pair_recv, tile_send, tile_recv):
    g = lax.axis_index("groups")
    t = lax.axis_index("train")
    q = lax.axis_index("query")
    f = lax.axis_index("feat")
    n_pool, width = train_pool.shape
    block_rows = train_pick.shape[0]
    step = width // CHUNKS
    load_train = pltpu.make_async_copy(train_pool, train_buf, local_sem.at[CHUNKS])
    load_train.start()
    loads = []
    for c in range(CHUNKS):
        cols = pl.ds(c * step, step)
        load = pltpu.make_async_copy(query_pool.at[:, cols], query_buf.at[:, cols], local_sem.at[c])
        load.start()
        loads.append(load)

    offsets = [
        (a, b, c) for a in range(n_train) for b in range(n_query) for c in range(n_feat)
    ][1:]

    def peer(a, b, c):
        return lax.rem(t + a, n_train), lax.rem(q + b, n_query), lax.rem(f + c, n_feat)

    def device(where):
        return (g, where[0], where[1], where[2])

    def place(where):
        return (where[0] * n_query + where[1]) * n_feat + where[2]

    barrier = pltpu.get_barrier_semaphore()
    for off in offsets:
        pl.semaphore_signal(
            barrier, inc=1, device_id=device(peer(*off)), device_id_type=pl.DeviceIdType.MESH
        )

    load_train.wait()
    for r in range(block_rows):
        named = jnp.clip(train_pick[r] - t * n_pool, 0, n_pool - 1)
        rows[r : r + 1, :] = train_buf[pl.ds(named, 1), :]
    pl.semaphore_wait(barrier, len(offsets))

    def remote(src, dst, send, recv, where):
        copy = pltpu.make_async_remote_copy(
            src_ref=src, dst_ref=dst, send_sem=send, recv_sem=recv,
            device_id=device(where), device_id_type=pl.DeviceIdType.MESH,
        )
        copy.start()
        return copy

    share = width // (n_train * n_query)
    a2a = []
    for a in range(1, n_train):
        where = peer(a, 0, 0)
        cols = pl.ds(pl.multiple_of((where[0] * n_query + q) * share, share), share)
        a2a.append(remote(rows.at[:, cols], blocks.at[t], a2a_send.at[a], a2a_recv.at[a], where))
    cols = pl.ds(pl.multiple_of((t * n_query + q) * share, share), share)
    blocks[t] = rows[:, cols]

    total = None
    for c in range(CHUNKS):
        loads[c].wait()
        term = dot_nt(rows[:, c * step : (c + 1) * step], query_buf[:, c * step : (c + 1) * step])
        total = term if total is None else total + term
    n_query_pool = query_pool.shape[0]
    n_queries = query_pick.shape[1]
    chosen = (
        lax.broadcasted_iota(jnp.int32, (n_query_pool, n_queries), 0)
        == query_pick[...] - q * n_query_pool
    ).astype(jnp.float32)
    mine[...] = jnp.dot(total, chosen, precision=HIGHEST, preferred_element_type=jnp.float32)
    pair = remote(mine, other, pair_send, pair_recv, peer(0, 0, 1))

    for copy in a2a:
        copy.wait()
    gathered = blocks[...].reshape(n_train * block_rows, share)
    part[...] = dot_nt(gathered, gathered)
    slab_rows = slab.shape[0]

    def slab_of(where):
        return pl.ds(pl.multiple_of(place(where) * slab_rows, slab_rows), slab_rows)

    here = (t, q, f)
    rs = []
    for i, off in enumerate(offsets):
        where = peer(*off)
        rs.append(remote(part.at[slab_of(where)], terms.at[i], rs_send.at[i], rs_recv.at[i], where))

    pair.wait()
    tile[...] = mine[...] + other[...]
    crosses[t] = tile[...]
    tiles = []
    for a in range(1, n_train):
        tiles.append(remote(tile, crosses.at[t], tile_send.at[a], tile_recv.at[a], peer(a, 0, 0)))

    for copy in rs:
        copy.wait()
    summed = part[slab_of(here), :]
    for i in range(len(offsets)):
        summed = summed + terms[i]
    slab[...] = summed
    full[slab_of(here), :] = summed
    ag = []
    for i, off in enumerate(offsets):
        ag.append(remote(slab, full.at[slab_of(here)], ag_send.at[i], ag_recv.at[i], peer(*off)))
    for copy in tiles:
        copy.wait()
    cross_out[...] = crosses[...].reshape(cross_out.shape)
    for copy in ag:
        copy.wait()
    kernel_out[...] = full[...]


def solve(kernel_ref, cross_ref, scores_ref, inverse):
    order = kernel_ref.shape[0]
    lane = lax.broadcasted_iota(jnp.int32, (8, order), 1)
    sub = lax.broadcasted_iota(jnp.int32, (8, order), 0)
    tiles = []
    for i in range(order // 8):
        diagonal = lane == sub + 8 * i
        tiles.append(kernel_ref[8 * i : 8 * i + 8, :] + jnp.where(diagonal, 0.5 * WIDTH, 0.0))
    for k in range(0, order, 2):
        home, r = k // 8, k % 8
        first = jnp.broadcast_to(tiles[home][r : r + 1, :], (8, order))
        second = jnp.broadcast_to(tiles[home][r + 1 : r + 2, :], (8, order))
        a = jnp.broadcast_to(first[:, k : k + 1], (8, order))
        b = jnp.broadcast_to(first[:, k + 1 : k + 2], (8, order))
        d = jnp.broadcast_to(second[:, k + 1 : k + 2], (8, order))
        inv_a = 1.0 / a
        ratio = b * inv_a
        inv_s = 1.0 / (d - b * ratio)
        at_k = lane == k
        at_k1 = lane == k + 1
        in_pair = at_k | at_k1
        first = jnp.where(in_pair, jnp.where(at_k, 1.0, 0.0), first)
        second = jnp.where(in_pair, jnp.where(at_k1, 1.0, 0.0), second)
        low = inv_s * (second - ratio * first)
        high = inv_a * first - ratio * low
        for i in range(order // 8):
            old = tiles[i]
            c0 = jnp.broadcast_to(old[:, k : k + 1], (8, order))
            c1 = jnp.broadcast_to(old[:, k + 1 : k + 2], (8, order))
            new = jnp.where(in_pair, 0.0, old) - c0 * high - c1 * low
            if i == home:
                new = jnp.where(sub == r, high, jnp.where(sub == r + 1, low, new))
            tiles[i] = new
    for i in range(order // 8):
        inverse[8 * i : 8 * i + 8, :] = tiles[i]
    columns = scores_ref.shape[1]
    start = pl.multiple_of(lax.axis_index("train") * columns, columns)
    scores_ref[...] = dot_nt(cross_ref[...].T, inverse[pl.ds(start, columns), :])


def with_kernels(sizes, train_pool, query_pool, train_pick, query_pick):
    n_train, n_query, n_feat = sizes
    n_peers = n_train * n_query * n_feat
    block_rows = train_pick.shape[0]
    order = block_rows * n_train
    n_queries = query_pick.shape[0]
    width = train_pool.shape[1]
    share = width // (n_train * n_query)
    slab_rows = order // n_peers
    vmem = pl.BlockSpec(memory_space=pltpu.VMEM)
    smem = pl.BlockSpec(memory_space=pltpu.SMEM)
    anywhere = pl.BlockSpec(memory_space=pl.ANY)
    f32 = jnp.float32
    dma = pltpu.SemaphoreType.DMA
    kernel, cross = pl.pallas_call(
        functools.partial(products, n_train, n_query, n_feat),
        out_shape=(
            jax.ShapeDtypeStruct((order, order), f32),
            jax.ShapeDtypeStruct((order, n_queries), f32),
        ),
        in_specs=[smem, vmem, anywhere, anywhere],
        out_specs=(vmem, vmem),
        scratch_shapes=[
            pltpu.VMEM(train_pool.shape, f32),
            pltpu.VMEM(query_pool.shape, f32),
            pltpu.VMEM((block_rows, width), f32),
            pltpu.VMEM((n_train, block_rows, share), f32),
            pltpu.VMEM((order, order), f32),
            pltpu.VMEM((n_peers - 1, slab_rows, order), f32),
            pltpu.VMEM((slab_rows, order), f32),
            pltpu.VMEM((order, order), f32),
            pltpu.VMEM((block_rows, n_queries), f32),
            pltpu.VMEM((block_rows, n_queries), f32),
            pltpu.VMEM((block_rows, n_queries), f32),
            pltpu.VMEM((n_train, block_rows, n_queries), f32),
            dma((CHUNKS + 1,)),
            dma((n_train,)), dma((n_train,)),
            dma((n_peers - 1,)), dma((n_peers - 1,)),
            dma((n_peers - 1,)), dma((n_peers - 1,)),
            dma, dma,
            dma((n_train,)), dma((n_train,)),
        ],
        compiler_params=pltpu.CompilerParams(
            collective_id=0, has_side_effects=True, vmem_limit_bytes=32 * 1024 * 1024
        ),
        name="products",
    )(train_pick, query_pick.reshape(1, n_queries), train_pool, query_pool)
    return pl.pallas_call(
        solve,
        out_shape=jax.ShapeDtypeStruct((n_queries, block_rows), f32),
        in_specs=[vmem, vmem],
        out_specs=vmem,
        scratch_shapes=[pltpu.VMEM((order, order), f32)],
        compiler_params=pltpu.CompilerParams(vmem_limit_bytes=32 * 1024 * 1024),
        name="solve",
    )(kernel, cross)


def with_arrays(train_pool, query_pool, train_pick, query_pick):
    block_rows = train_pick.shape[0]
    train_index = lax.axis_index("train")
    query_index = lax.axis_index("query")
    train_rows = jnp.take(train_pool, train_pick - train_index * train_pool.shape[0], axis=0)
    query_rows = jnp.take(query_pool, query_pick - query_index * query_pool.shape[0], axis=0)
    cross_tile = dot_nt(query_rows, train_rows)
    kernel_part = dot_nt(train_rows, lax.all_gather(train_rows, "train", axis=0, tiled=True))
    cross_tile, kernel_part = lax.psum((cross_tile, kernel_part), "feat")
    kernel = lax.all_gather(kernel_part, "train", axis=0, tiled=True)
    order = kernel.shape[0]
    factor = jnp.linalg.cholesky(kernel + 0.5 * WIDTH * jnp.eye(order, dtype=jnp.float32))
    sel_rows = lax.broadcasted_iota(jnp.int32, (order, block_rows), 0)
    sel_cols = lax.broadcasted_iota(jnp.int32, (order, block_rows), 1) + train_index * block_rows
    selector = (sel_rows == sel_cols).astype(jnp.float32)
    halfway = lax.linalg.triangular_solve(factor, selector, left_side=True, lower=True)
    inverse_cols = lax.linalg.triangular_solve(
        factor, halfway, left_side=True, lower=True, transpose_a=True
    )
    return jnp.dot(
        lax.all_gather(cross_tile, "train", axis=1, tiled=True),
        inverse_cols,
        precision=HIGHEST,
        preferred_element_type=jnp.float32,
    )


def solution(mesh):
    sizes = mesh.shape["train"], mesh.shape["query"], mesh.shape["feat"]

    def on_device(train_pool, query_pool, train_pick, query_pick):
        order = train_pick.shape[0] * sizes[0]
        fits = (
            order == 128
            and order % (8 * sizes[0] * sizes[1] * sizes[2]) == 0
            and train_pool.shape[1] % (128 * sizes[0] * sizes[1]) == 0
        )
        if fits:
            return with_kernels(sizes, train_pool, query_pool, train_pick, query_pick)
        return with_arrays(train_pool, query_pool, train_pick, query_pick)

    return jax.shard_map(
        on_device,
        mesh=mesh,
        in_specs=(
            P(("groups", "train"), "feat"),
            P(("groups", "query"), "feat"),
            P(("groups", "train")),
            P(("groups", "query")),
        ),
        out_specs=P(("groups", "query"), "train"),
        check_vma=False,
    )
```

time: 142 us -> 41.1 us (0.29)
  waiting for transfers between devices: 39.5 us -> 0 us
  Pallas kernels: 0 us -> 35.8 us
  other arithmetic: 33.6 us -> 0 us
  blocking collectives: 32.5 us -> 0 us
  between operations: 13.5 us -> 0.02 us
  matrix products: 13.3 us -> 0 us
  local copies, waits for them, and re-layouts: 8.43 us -> 5.11 us
    all_gather x1 -> x0, waiting for transfers between devices: 39.5 us -> none  [on_device(): lax.all_gather(train_rows, 'train', axis=0, tiled=True)]
    pallas_call x0 -> x2, Pallas kernels: none -> 35.8 us  [the longest x1 24.9 us: with_kernels(): pl.pallas_call(functools.partial(products, n_train, n_query, n_feat), out...]
    another operation x5 -> x0, other arithmetic: 28.1 us -> none  [the longest x3 14.7 us: on_device(): factor = jnp.linalg.cholesky(kernel + 0.5 * WIDTH * identity)]
    all_gather x2 -> x0, blocking collectives: 27.8 us -> none  [the longest x1 14.3 us: on_device(): lax.all_gather(cross_tile, 'train', axis=1, tiled=True)]
    dot_general x3 -> x0, matrix products: 11.2 us -> none  [the longest x1 5.51 us: on_device(): jnp.dot(query_rows, train_rows.T, precision=highest, preferred_element_ty...]
    gather x2 -> x0, local copies, waits for them, and re-layouts: 6.23 us -> none  [the longest x1 3.22 us: on_device(): jnp.take(query_pool, query_pick - query_index * query_pool.shape[0], axis=0)]
    psum x1 -> x0, blocking collectives: 4.68 us -> none  [on_device(): cross_tile, kernel_part = lax.psum((cross_tile, kernel_part), 'feat')]
    unnamed x6 -> x8, local copies, waits for them, and re-layouts: 0.64 us -> 4.42 us
  transfers between devices with their start and end apart: 1 -> 0, of which waited for: 1 -> 0; matrix products, arithmetic and copies ran while one was open for 7% -> 0% of each run, Pallas kernels for 0% -> 0%
where the time goes in v1:
time: 41.1 us; the launch traced here: 40.9 us
  Pallas kernels  35.8 us (87%)
  local copies, waits for them, and re-layouts  5.11 us (12%)
    pallas_call x1, Pallas kernels, with_kernels(): pl.pallas_call(functools.partial(products, n_train, n_query, n_feat), out...  24.9 us
    pallas_call x1, Pallas kernels, with_kernels(): pl.pallas_call(solve, out_shape=jax.ShapeDtypeStruct((n_queries, block_ro...  10.9 us
    unnamed x8, local copies, waits for them, and re-layouts  4.42 us

profile of v1, /device:TPU:0, one launch (start us, length us, event | category | flops | bytes accessed | tf_op | source)
XLA Modules:
  0.0 40.9 jit_solution(12658100460421186771)
XLA Ops:
  0.0 0.0 copy-start
  0.0 2.0 %copy-done = f32[216,4096]{1,0:T(8,128)S(1)} copy-done((f32[216,4096]{1,0:T(8,128)S(1)}, f32[216,4096]{1,0:T(8,128)}, u32[]{:S(2)}) %copy-start) | copy-done | bytes 3538968
  2.0 0.0 copy-start.1
  2.0 1.1 %copy-done.1 = f32[40,4096]{1,0:T(8,128)S(1)} copy-done((f32[40,4096]{1,0:T(8,128)S(1)}, f32[40,4096]{1,0:T(8,128)}, u32[]{:S(2)}) %copy-start.1) | copy-done | bytes 655384
  3.1 0.0 copy-start.2
  3.1 0.7 %copy-done.2 = s32[192]{0:T(256)S(1)} copy-done((s32[192]{0:T(256)S(1)}, s32[192]{0:T(256)}, u32[]{:S(2)}) %copy-start.2) | copy-done | bytes 792
  3.8 0.0 copy-start.3
  3.8 0.7 %copy-done.3 = s32[32]{0:T(128)S(1)} copy-done((s32[32]{0:T(128)S(1)}, s32[32]{0:T(128)}, u32[]{:S(2)}) %copy-start.3) | copy-done | bytes 152
  4.4 24.9 %products.1 = (f32[128,128]{1,0:T(8,128)S(1)}, f32[128,192]{1,0:T(8,128)S(1)}) custom-call(s32[32]{0:T(128)S(1)} %copy-done.3, s32[1,192]{1,0:T(1,128)S(1)} %bitcast.1, f32[40,4096]{1,0:T(8,128)S(1)} %copy-done.1, f32[216,4096]{1,0:T(8,128)S(1)} %copy-done), custom_call_target="tpu_custom_call" | custom-call | tf_op jit(solution)/shard_map/products/pallas_call | solution.py:191
  29.3 10.9 %solve.1 = f32[192,32]{1,0:T(8,128)S(1)} custom-call(f32[128,128]{1,0:T(8,128)S(1)} %get-tuple-element.7.kernel_ref, f32[128,192]{1,0:T(8,128)S(1)} %get-tuple-element.8.cross_ref), custom_call_target="tpu_custom_call" | custom-call | tf_op jit(solution)/shard_map/solve/pallas_call | solution.py:224
  40.2 0.7 %copy.5 = f32[192,32]{0,1:T(8,128)} copy(f32[192,32]{1,0:T(8,128)S(1)} %solve.1) | data formatting | bytes 49152 | tf_op jit(solution)/shard_map/solve/pallas_call | solution.py:224
Async XLA Ops:
  0.0 2.0 %copy-start = (f32[216,4096]{1,0:T(8,128)S(1)}, f32[216,4096]{1,0:T(8,128)}, u32[]{:S(2)}) copy-start(f32[216,4096]{1,0:T(8,128)} %query_pool.1) | copy-start | bytes 10616836
  2.0 1.1 %copy-start.1 = (f32[40,4096]{1,0:T(8,128)S(1)}, f32[40,4096]{1,0:T(8,128)}, u32[]{:S(2)}) copy-start(f32[40,4096]{1,0:T(8,128)} %train_pool.1) | copy-start | bytes 1966084
  3.1 0.7 %copy-start.2 = (s32[192]{0:T(256)S(1)}, s32[192]{0:T(256)}, u32[]{:S(2)}) copy-start(s32[192]{0:T(256)} %param.7) | copy-start | bytes 2308
  3.8 0.7 %copy-start.3 = (s32[32]{0:T(128)S(1)}, s32[32]{0:T(128)}, u32[]{:S(2)}) copy-start(s32[32]{0:T(128)} %train_pick.1) | copy-start | bytes 388

commit v2 on v1

--- a/solution.py
+++ b/solution.py
@@ -17,8 +17,8 @@
     return lax.dot_general(a, b, NT, precision=HIGHEST, preferred_element_type=jnp.float32)
 
 
-def products(n_train, n_query, n_feat, train_pick, query_pick, train_pool, query_pool,
-             kernel_out, cross_out,
+def products(n_train, n_query, n_feat, train_pick_in, query_pick_in, train_pool, query_pool,
+             kernel_out, cross_out, train_pick, query_pick,
              train_buf, query_buf, rows, blocks, part, terms, slab, full, mine, other, tile, crosses,
              local_sem, a2a_send, a2a_recv, rs_send, rs_recv, ag_send, ag_recv,
              pair_send, pair_recv, tile_send, tile_recv):
@@ -31,6 +31,12 @@
     step = width // CHUNKS
     load_train = pltpu.make_async_copy(train_pool, train_buf, local_sem.at[CHUNKS])
     load_train.start()
+    load_picks = [
+        pltpu.make_async_copy(train_pick_in, train_pick, local_sem.at[CHUNKS + 1]),
+        pltpu.make_async_copy(query_pick_in, query_pick, local_sem.at[CHUNKS + 2]),
+    ]
+    for load in load_picks:
+        load.start()
     loads = []
     for c in range(CHUNKS):
         cols = pl.ds(c * step, step)
@@ -57,6 +63,8 @@
             barrier, inc=1, device_id=device(peer(*off)), device_id_type=pl.DeviceIdType.MESH
         )
 
+    for load in load_picks:
+        load.wait()
     load_train.wait()
     for r in range(block_rows):
         named = jnp.clip(train_pick[r] - t * n_pool, 0, n_pool - 1)
@@ -169,9 +177,12 @@
             tiles[i] = new
     for i in range(order // 8):
         inverse[8 * i : 8 * i + 8, :] = tiles[i]
-    columns = scores_ref.shape[1]
+    columns = scores_ref.shape[0]
     start = pl.multiple_of(lax.axis_index("train") * columns, columns)
-    scores_ref[...] = dot_nt(cross_ref[...].T, inverse[pl.ds(start, columns), :])
+    scores_ref[...] = jnp.dot(
+        inverse[pl.ds(start, columns), :], cross_ref[...],
+        precision=HIGHEST, preferred_element_type=jnp.float32,
+    )
 
 
 def with_kernels(sizes, train_pool, query_pool, train_pick, query_pick):
@@ -184,8 +195,7 @@
     share = width // (n_train * n_query)
     slab_rows = order // n_peers
     vmem = pl.BlockSpec(memory_space=pltpu.VMEM)
-    smem = pl.BlockSpec(memory_space=pltpu.SMEM)
-    anywhere = pl.BlockSpec(memory_space=pl.ANY)
+    hbm = pl.BlockSpec(memory_space=pltpu.HBM)
     f32 = jnp.float32
     dma = pltpu.SemaphoreType.DMA
     kernel, cross = pl.pallas_call(
@@ -194,9 +204,11 @@
             jax.ShapeDtypeStruct((order, order), f32),
             jax.ShapeDtypeStruct((order, n_queries), f32),
         ),
-        in_specs=[smem, vmem, anywhere, anywhere],
+        in_specs=[hbm] * 4,
         out_specs=(vmem, vmem),
         scratch_shapes=[
+            pltpu.SMEM((block_rows,), jnp.int32),
+            pltpu.VMEM((1, n_queries), jnp.int32),
             pltpu.VMEM(train_pool.shape, f32),
             pltpu.VMEM(query_pool.shape, f32),
             pltpu.VMEM((block_rows, width), f32),
@@ -209,7 +221,7 @@
             pltpu.VMEM((block_rows, n_queries), f32),
             pltpu.VMEM((block_rows, n_queries), f32),
             pltpu.VMEM((n_train, block_rows, n_queries), f32),
-            dma((CHUNKS + 1,)),
+            dma((CHUNKS + 3,)),
             dma((n_train,)), dma((n_train,)),
             dma((n_peers - 1,)), dma((n_peers - 1,)),
             dma((n_peers - 1,)), dma((n_peers - 1,)),
@@ -223,13 +235,13 @@
     )(train_pick, query_pick.reshape(1, n_queries), train_pool, query_pool)
     return pl.pallas_call(
         solve,
-        out_shape=jax.ShapeDtypeStruct((n_queries, block_rows), f32),
+        out_shape=jax.ShapeDtypeStruct((block_rows, n_queries), f32),
         in_specs=[vmem, vmem],
         out_specs=vmem,
         scratch_shapes=[pltpu.VMEM((order, order), f32)],
         compiler_params=pltpu.CompilerParams(vmem_limit_bytes=32 * 1024 * 1024),
         name="solve",
-    )(kernel, cross)
+    )(kernel, cross).T
 
 
 def with_arrays(train_pool, query_pool, train_pick, query_pick):

time: 41.1 us -> 40.5 us (0.985)
  local copies, waits for them, and re-layouts: 5.11 us -> 4.42 us
    pallas_call x1 -> x0, local copies, waits for them, and re-layouts: 0.69 us -> none  [with_kernels(): pl.pallas_call(solve, out_shape=jax.ShapeDtypeStruct((n_queries, block_ro...]
    pallas_call x1, Pallas kernels: 10.9 us -> 11.5 us  [with_kernels(): pl.pallas_call(solve, out_shape=jax.ShapeDtypeStruct((block_rows, n_queri...]
    pallas_call x1, Pallas kernels: 24.9 us -> 24.3 us  [with_kernels(): pl.pallas_call(functools.partial(products, n_train, n_query, n_feat), out...]
where the time goes in v2:
time: 40.5 us; the launch traced here: 40.3 us
  Pallas kernels  35.9 us (89%)
  local copies, waits for them, and re-layouts  4.42 us (11%)
    pallas_call x1, Pallas kernels, with_kernels(): pl.pallas_call(functools.partial(products, n_train, n_query, n_feat), out...  24.3 us
    pallas_call x1, Pallas kernels, with_kernels(): pl.pallas_call(solve, out_shape=jax.ShapeDtypeStruct((block_rows, n_queri...  11.5 us
    unnamed x8, local copies, waits for them, and re-layouts  4.42 us

profile of v2, /device:TPU:0, one launch (start us, length us, event | category | flops | bytes accessed | tf_op | source)
XLA Modules:
  0.0 40.3 jit_solution(5548980494549525519)
XLA Ops:
  0.0 0.0 copy-start
  0.0 2.0 %copy-done = f32[216,4096]{1,0:T(8,128)S(1)} copy-done((f32[216,4096]{1,0:T(8,128)S(1)}, f32[216,4096]{1,0:T(8,128)}, u32[]{:S(2)}) %copy-start) | copy-done | bytes 3538968
  2.0 0.0 copy-start.1
  2.0 1.1 %copy-done.1 = f32[40,4096]{1,0:T(8,128)S(1)} copy-done((f32[40,4096]{1,0:T(8,128)S(1)}, f32[40,4096]{1,0:T(8,128)}, u32[]{:S(2)}) %copy-start.1) | copy-done | bytes 655384
  3.1 0.0 copy-start.2
  3.1 0.7 %copy-done.2 = s32[192]{0:T(256)S(1)} copy-done((s32[192]{0:T(256)S(1)}, s32[192]{0:T(256)}, u32[]{:S(2)}) %copy-start.2) | copy-done | bytes 792
  3.8 0.0 copy-start.3
  3.8 0.7 %copy-done.3 = s32[32]{0:T(128)S(1)} copy-done((s32[32]{0:T(128)S(1)}, s32[32]{0:T(128)}, u32[]{:S(2)}) %copy-start.3) | copy-done | bytes 152
  4.4 24.3 %products.1 = (f32[128,128]{1,0:T(8,128)S(1)}, f32[128,192]{1,0:T(8,128)S(1)}) custom-call(s32[32]{0:T(128)S(1)} %copy-done.3, s32[1,192]{1,0:T(1,128)S(1)} %bitcast.2, f32[40,4096]{1,0:T(8,128)S(1)} %copy-done.1, f32[216,4096]{1,0:T(8,128)S(1)} %copy-done), custom_call_target="tpu_custom_call" | custom-call | tf_op jit(solution)/shard_map/products/pallas_call | solution.py:201
  28.8 11.5 %solve.1 = f32[32,192]{1,0:T(8,128)} custom-call(f32[128,128]{1,0:T(8,128)S(1)} %get-tuple-element.7.kernel_ref, f32[128,192]{1,0:T(8,128)S(1)} %get-tuple-element.8.cross_ref), custom_call_target="tpu_custom_call" | custom-call | tf_op jit(solution)/shard_map/solve/pallas_call | solution.py:236
Async XLA Ops:
  0.0 2.0 %copy-start = (f32[216,4096]{1,0:T(8,128)S(1)}, f32[216,4096]{1,0:T(8,128)}, u32[]{:S(2)}) copy-start(f32[216,4096]{1,0:T(8,128)} %query_pool.1) | copy-start | bytes 10616836
  2.0 1.1 %copy-start.1 = (f32[40,4096]{1,0:T(8,128)S(1)}, f32[40,4096]{1,0:T(8,128)}, u32[]{:S(2)}) copy-start(f32[40,4096]{1,0:T(8,128)} %train_pool.1) | copy-start | bytes 1966084
  3.1 0.7 %copy-start.2 = (s32[192]{0:T(256)S(1)}, s32[192]{0:T(256)}, u32[]{:S(2)}) copy-start(s32[192]{0:T(256)} %param.7) | copy-start | bytes 2308
  3.8 0.7 %copy-start.3 = (s32[32]{0:T(128)S(1)}, s32[32]{0:T(128)}, u32[]{:S(2)}) copy-start(s32[32]{0:T(128)} %train_pick_in.1) | copy-start | bytes 388

commit v3 on v2

--- a/solution.py
+++ b/solution.py
@@ -17,9 +17,51 @@
     return lax.dot_general(a, b, NT, precision=HIGHEST, preferred_element_type=jnp.float32)
 
 
+def halves(x):
+    high = x.astype(jnp.bfloat16)
+    return high, (x - high.astype(jnp.float32)).astype(jnp.bfloat16)
+
+
+def invert(kernel_ref, inverse):
+    order = kernel_ref.shape[0]
+    lane = lax.broadcasted_iota(jnp.int32, (8, order), 1)
+    sub = lax.broadcasted_iota(jnp.int32, (8, order), 0)
+    tiles = []
+    for i in range(order // 8):
+        diagonal = lane == sub + 8 * i
+        tiles.append(kernel_ref[8 * i : 8 * i + 8, :] + jnp.where(diagonal, 0.5 * WIDTH, 0.0))
+    for k in range(0, order, 2):
+        home, r = k // 8, k % 8
+        first = jnp.broadcast_to(tiles[home][r : r + 1, :], (8, order))
+        second = jnp.broadcast_to(tiles[home][r + 1 : r + 2, :], (8, order))
+        a = jnp.broadcast_to(first[:, k : k + 1], (8, order))
+        b = jnp.broadcast_to(first[:, k + 1 : k + 2], (8, order))
+        d = jnp.broadcast_to(second[:, k + 1 : k + 2], (8, order))
+        scale = 1.0 / (a * d - b * b)
+        a, b, d = a * scale, b * scale, d * scale
+        at_k = lane == k
+        at_k1 = lane == k + 1
+        in_pair = at_k | at_k1
+        first = jnp.where(in_pair, jnp.where(at_k, 1.0, 0.0), first)
+        second = jnp.where(in_pair, jnp.where(at_k1, 1.0, 0.0), second)
+        high = d * first - b * second
+        low = a * second - b * first
+        following = min(k + 2, order - 1) // 8
+        for i in sorted(range(order // 8), key=lambda i: i != following):
+            old = tiles[i]
+            c0 = jnp.broadcast_to(old[:, k : k + 1], (8, order))
+            c1 = jnp.broadcast_to(old[:, k + 1 : k + 2], (8, order))
+            new = jnp.where(in_pair, 0.0, old) - c0 * high - c1 * low
+            if i == home:
+                new = jnp.where(sub == r, high, jnp.where(sub == r + 1, low, new))
+            tiles[i] = new
+    for i in range(order // 8):
+        inverse[8 * i : 8 * i + 8, :] = tiles[i]
+
+
 def products(n_train, n_query, n_feat, train_pick_in, query_pick_in, train_pool, query_pool,
-             kernel_out, cross_out, train_pick, query_pick,
-             train_buf, query_buf, rows, blocks, part, terms, slab, full, mine, other, tile, crosses,
+             scores_out, train_pick, query_pick,
+             train_buf, query_buf, rows, blocks, part, terms, slab, full, inverse, mine, other, tile, crosses,
              local_sem, a2a_send, a2a_recv, rs_send, rs_recv, ag_send, ag_recv,
              pair_send, pair_recv, tile_send, tile_recv):
     g = lax.axis_index("groups")
@@ -91,7 +133,16 @@
     total = None
     for c in range(CHUNKS):
         loads[c].wait()
-        term = dot_nt(rows[:, c * step : (c + 1) * step], query_buf[:, c * step : (c + 1) * step])
+        cols = slice(c * step, (c + 1) * step)
+        x_high, x_low = halves(rows[:, cols])
+        y_high, y_low = halves(query_buf[:, cols])
+        both = lax.dot_general(
+            jnp.concatenate([x_high, x_low]), y_high, NT, preferred_element_type=jnp.float32
+        )
+        term = both[:block_rows] + (
+            both[block_rows:]
+            + lax.dot_general(x_high, y_low, NT, preferred_element_type=jnp.float32)
+        )
         total = term if total is None else total + term
     n_query_pool = query_pool.shape[0]
     n_queries = query_pick.shape[1]
@@ -134,54 +185,17 @@
     ag = []
     for i, off in enumerate(offsets):
         ag.append(remote(slab, full.at[slab_of(here)], ag_send.at[i], ag_recv.at[i], peer(*off)))
+    for copy in ag:
+        copy.wait()
+    invert(full, inverse)
     for copy in tiles:
         copy.wait()
-    cross_out[...] = crosses[...].reshape(cross_out.shape)
-    for copy in ag:
-        copy.wait()
-    kernel_out[...] = full[...]
-
-
-def solve(kernel_ref, cross_ref, scores_ref, inverse):
-    order = kernel_ref.shape[0]
-    lane = lax.broadcasted_iota(jnp.int32, (8, order), 1)
-    sub = lax.broadcasted_iota(jnp.int32, (8, order), 0)
-    tiles = []
-    for i in range(order // 8):
-        diagonal = lane == sub + 8 * i
-        tiles.append(kernel_ref[8 * i : 8 * i + 8, :] + jnp.where(diagonal, 0.5 * WIDTH, 0.0))
-    for k in range(0, order, 2):
-        home, r = k // 8, k % 8
-        first = jnp.broadcast_to(tiles[home][r : r + 1, :], (8, order))
-        second = jnp.broadcast_to(tiles[home][r + 1 : r + 2, :], (8, order))
-        a = jnp.broadcast_to(first[:, k : k + 1], (8, order))
-        b = jnp.broadcast_to(first[:, k + 1 : k + 2], (8, order))
-        d = jnp.broadcast_to(second[:, k + 1 : k + 2], (8, order))
-        inv_a = 1.0 / a
-        ratio = b * inv_a
-        inv_s = 1.0 / (d - b * ratio)
-        at_k = lane == k
-        at_k1 = lane == k + 1
-        in_pair = at_k | at_k1
-        first = jnp.where(in_pair, jnp.where(at_k, 1.0, 0.0), first)
-        second = jnp.where(in_pair, jnp.where(at_k1, 1.0, 0.0), second)
-        low = inv_s * (second - ratio * first)
-        high = inv_a * first - ratio * low
-        for i in range(order // 8):
-            old = tiles[i]
-            c0 = jnp.broadcast_to(old[:, k : k + 1], (8, order))
-            c1 = jnp.broadcast_to(old[:, k + 1 : k + 2], (8, order))
-            new = jnp.where(in_pair, 0.0, old) - c0 * high - c1 * low
-            if i == home:
-                new = jnp.where(sub == r, high, jnp.where(sub == r + 1, low, new))
-            tiles[i] = new
-    for i in range(order // 8):
-        inverse[8 * i : 8 * i + 8, :] = tiles[i]
-    columns = scores_ref.shape[0]
-    start = pl.multiple_of(lax.axis_index("train") * columns, columns)
-    scores_ref[...] = jnp.dot(
-        inverse[pl.ds(start, columns), :], cross_ref[...],
-        precision=HIGHEST, preferred_element_type=jnp.float32,
+    start = pl.multiple_of(t * block_rows, block_rows)
+    scores_out[...] = jnp.dot(
+        inverse[pl.ds(start, block_rows), :],
+        crosses[...].reshape(n_train * block_rows, n_queries),
+        precision=HIGHEST,
+        preferred_element_type=jnp.float32,
     )
 
 
@@ -198,14 +212,11 @@
     hbm = pl.BlockSpec(memory_space=pltpu.HBM)
     f32 = jnp.float32
     dma = pltpu.SemaphoreType.DMA
-    kernel, cross = pl.pallas_call(
+    scores = pl.pallas_call(
         functools.partial(products, n_train, n_query, n_feat),
-        out_shape=(
-            jax.ShapeDtypeStruct((order, order), f32),
-            jax.ShapeDtypeStruct((order, n_queries), f32),
-        ),
+        out_shape=jax.ShapeDtypeStruct((block_rows, n_queries), f32),
         in_specs=[hbm] * 4,
-        out_specs=(vmem, vmem),
+        out_specs=vmem,
         scratch_shapes=[
             pltpu.SMEM((block_rows,), jnp.int32),
             pltpu.VMEM((1, n_queries), jnp.int32),
@@ -216,6 +227,7 @@
             pltpu.VMEM((order, order), f32),
             pltpu.VMEM((n_peers - 1, slab_rows, order), f32),
             pltpu.VMEM((slab_rows, order), f32),
+            pltpu.VMEM((order, order), f32),
             pltpu.VMEM((order, order), f32),
             pltpu.VMEM((block_rows, n_queries), f32),
             pltpu.VMEM((block_rows, n_queries), f32),
@@ -229,19 +241,11 @@
             dma((n_train,)), dma((n_train,)),
         ],
         compiler_params=pltpu.CompilerParams(
-            collective_id=0, has_side_effects=True, vmem_limit_bytes=32 * 1024 * 1024
+            collective_id=0, has_side_effects=True, vmem_limit_bytes=64 * 1024 * 1024
         ),
         name="products",
     )(train_pick, query_pick.reshape(1, n_queries), train_pool, query_pool)
-    return pl.pallas_call(
-        solve,
-        out_shape=jax.ShapeDtypeStruct((block_rows, n_queries), f32),
-        in_specs=[vmem, vmem],
-        out_specs=vmem,
-        scratch_shapes=[pltpu.VMEM((order, order), f32)],
-        compiler_params=pltpu.CompilerParams(vmem_limit_bytes=32 * 1024 * 1024),
-        name="solve",
-    )(kernel, cross).T
+    return scores.T
 
 
 def with_arrays(train_pool, query_pool, train_pick, query_pick):

time: 40.5 us -> 35.8 us (0.88)
  local copies, waits for them, and re-layouts: 4.42 us -> 1.38 us
  Pallas kernels: 35.9 us -> 34.2 us
    pallas_call x1 -> x0, Pallas kernels: 11.5 us -> none  [with_kernels(): pl.pallas_call(solve, out_shape=jax.ShapeDtypeStruct((block_rows, n_queri...]
    pallas_call x1, Pallas kernels: 24.3 us -> 34.2 us  [with_kernels(): pl.pallas_call(functools.partial(products, n_train, n_query, n_feat), out...]
    unnamed x8 -> x1, local copies, waits for them, and re-layouts: 4.42 us -> 1.38 us
where the time goes in v3:
time: 35.8 us; the launch traced here: 35.6 us
  Pallas kernels  34.2 us (96%)
  local copies, waits for them, and re-layouts  1.38 us (4%)
    pallas_call x1, Pallas kernels, with_kernels(): pl.pallas_call(functools.partial(products, n_train, n_query, n_feat), out...  34.2 us
    unnamed x1, local copies, waits for them, and re-layouts  1.38 us

profile of v3, /device:TPU:0, one launch (start us, length us, event | category | flops | bytes accessed | tf_op | source)
XLA Modules:
  0.0 35.6 jit_solution(1005309601567147667)
XLA Ops:
  0.0 34.2 %products.1 = f32[32,192]{1,0:T(8,128)} custom-call(s32[32]{0:T(128)} %train_pick_in.1, s32[1,192]{1,0:T(1,128)} %bitcast.3, f32[40,4096]{1,0:T(8,128)} %train_pool.1, f32[216,4096]{1,0:T(8,128)} %query_pool.1), custom_call_target="tpu_custom_call" | custom-call | tf_op jit(solution)/shard_map/products/pallas_call | solution.py:215
  34.2 1.4 %copy.6 = f32[192,32]{0,1:T(8,128)} copy(f32[192,32]{0,1:T(8,128)} %bitcast.2) | data formatting | bytes 49152

commit v4 on v3

--- a/solution.py
+++ b/solution.py
@@ -17,9 +17,17 @@
     return lax.dot_general(a, b, NT, precision=HIGHEST, preferred_element_type=jnp.float32)
 
 
-def halves(x):
+def parts(x):
     high = x.astype(jnp.bfloat16)
-    return high, (x - high.astype(jnp.float32)).astype(jnp.bfloat16)
+    rest = x - high.astype(jnp.float32)
+    middle = rest.astype(jnp.bfloat16)
+    low = (rest - middle.astype(jnp.float32)).astype(jnp.bfloat16)
+    return high, middle, low
+
+
+def inverse_2x2(a, b, d):
+    scale = 1.0 / (a * d - b * b)
+    return d * scale, -b * scale, a * scale
 
 
 def invert(kernel_ref, inverse):
@@ -30,30 +38,47 @@
     for i in range(order // 8):
         diagonal = lane == sub + 8 * i
         tiles.append(kernel_ref[8 * i : 8 * i + 8, :] + jnp.where(diagonal, 0.5 * WIDTH, 0.0))
-    for k in range(0, order, 2):
+
+    def columns(tile, k):
+        return [jnp.broadcast_to(tile[:, k + j : k + j + 1], (8, order)) for j in range(4)]
+
+    def row(tile, r):
+        return jnp.broadcast_to(tile[r : r + 1, :], (8, order))
+
+    for k in range(0, order, 4):
         home, r = k // 8, k % 8
-        first = jnp.broadcast_to(tiles[home][r : r + 1, :], (8, order))
-        second = jnp.broadcast_to(tiles[home][r + 1 : r + 2, :], (8, order))
-        a = jnp.broadcast_to(first[:, k : k + 1], (8, order))
-        b = jnp.broadcast_to(first[:, k + 1 : k + 2], (8, order))
-        d = jnp.broadcast_to(second[:, k + 1 : k + 2], (8, order))
-        scale = 1.0 / (a * d - b * b)
-        a, b, d = a * scale, b * scale, d * scale
-        at_k = lane == k
-        at_k1 = lane == k + 1
-        in_pair = at_k | at_k1
-        first = jnp.where(in_pair, jnp.where(at_k, 1.0, 0.0), first)
-        second = jnp.where(in_pair, jnp.where(at_k1, 1.0, 0.0), second)
-        high = d * first - b * second
-        low = a * second - b * first
-        following = min(k + 2, order - 1) // 8
+        pivots = columns(tiles[home], k)
+        a00, a01, a02, a03 = (row(pivots[j], r) for j in range(4))
+        a11, a12, a13 = (row(pivots[j], r + 1) for j in range(1, 4))
+        a22, a23 = (row(pivots[j], r + 2) for j in range(2, 4))
+        a33 = row(pivots[3], r + 3)
+        in_pivot = (lane >= k) & (lane < k + 4)
+        r0, r1, r2, r3 = (
+            jnp.where(in_pivot, jnp.where(lane == k + j, 1.0, 0.0), row(tiles[home], r + j))
+            for j in range(4)
+        )
+        d00, d01, d11 = inverse_2x2(a00, a01, a11)
+        x00, x01 = d00 * a02 + d01 * a12, d00 * a03 + d01 * a13
+        x10, x11 = d01 * a02 + d11 * a12, d01 * a03 + d11 * a13
+        e00, e01, e11 = inverse_2x2(
+            a22 - (a02 * x00 + a12 * x10),
+            a23 - (a02 * x01 + a12 * x11),
+            a33 - (a03 * x01 + a13 * x11),
+        )
+        v2 = r2 - (x00 * r0 + x10 * r1)
+        v3 = r3 - (x01 * r0 + x11 * r1)
+        w2 = e00 * v2 + e01 * v3
+        w3 = e01 * v2 + e11 * v3
+        w0 = (d00 * r0 + d01 * r1) - (x00 * w2 + x01 * w3)
+        w1 = (d01 * r0 + d11 * r1) - (x10 * w2 + x11 * w3)
+        following = min(k + 4, order - 1) // 8
         for i in sorted(range(order // 8), key=lambda i: i != following):
-            old = tiles[i]
-            c0 = jnp.broadcast_to(old[:, k : k + 1], (8, order))
-            c1 = jnp.broadcast_to(old[:, k + 1 : k + 2], (8, order))
-            new = jnp.where(in_pair, 0.0, old) - c0 * high - c1 * low
+            c = pivots if i == home else columns(tiles[i], k)
+            new = jnp.where(in_pivot, 0.0, tiles[i])
+            new = new - ((c[0] * w0 + c[1] * w1) + (c[2] * w2 + c[3] * w3))
             if i == home:
-                new = jnp.where(sub == r, high, jnp.where(sub == r + 1, low, new))
+                for j, w in enumerate((w0, w1, w2, w3)):
+                    new = jnp.where(sub == r + j, w, new)
             tiles[i] = new
     for i in range(order // 8):
         inverse[8 * i : 8 * i + 8, :] = tiles[i]
@@ -108,9 +133,18 @@
     for load in load_picks:
         load.wait()
     load_train.wait()
-    for r in range(block_rows):
-        named = jnp.clip(train_pick[r] - t * n_pool, 0, n_pool - 1)
-        rows[r : r + 1, :] = train_buf[pl.ds(named, 1), :]
+    named = [jnp.clip(train_pick[r] - t * n_pool, 0, n_pool - 1) for r in range(block_rows)]
+    share = width // (n_train * n_query)
+
+    def share_of(a, b):
+        where = peer(a, b, 0)
+        return pl.ds(pl.multiple_of((where[0] * n_query + where[1]) * share, share), share)
+
+    def select(cols):
+        for r in range(block_rows):
+            rows[r : r + 1, cols] = train_buf[pl.ds(named[r], 1), cols]
+
+    select(share_of(1, 0))
     pl.semaphore_wait(barrier, len(offsets))
 
     def remote(src, dst, send, recv, where):
@@ -121,28 +155,33 @@
         copy.start()
         return copy
 
-    share = width // (n_train * n_query)
     a2a = []
     for a in range(1, n_train):
-        where = peer(a, 0, 0)
-        cols = pl.ds(pl.multiple_of((where[0] * n_query + q) * share, share), share)
-        a2a.append(remote(rows.at[:, cols], blocks.at[t], a2a_send.at[a], a2a_recv.at[a], where))
-    cols = pl.ds(pl.multiple_of((t * n_query + q) * share, share), share)
-    blocks[t] = rows[:, cols]
+        cols = share_of(a, 0)
+        if a > 1:
+            select(cols)
+        a2a.append(
+            remote(rows.at[:, cols], blocks.at[t], a2a_send.at[a], a2a_recv.at[a], peer(a, 0, 0))
+        )
+    select(share_of(0, 0))
+    blocks[t] = rows[:, share_of(0, 0)]
+    for a in range(n_train):
+        for b in range(1, n_query):
+            select(share_of(a, b))
 
     total = None
     for c in range(CHUNKS):
         loads[c].wait()
         cols = slice(c * step, (c + 1) * step)
-        x_high, x_low = halves(rows[:, cols])
-        y_high, y_low = halves(query_buf[:, cols])
-        both = lax.dot_general(
-            jnp.concatenate([x_high, x_low]), y_high, NT, preferred_element_type=jnp.float32
-        )
-        term = both[:block_rows] + (
-            both[block_rows:]
-            + lax.dot_general(x_high, y_low, NT, preferred_element_type=jnp.float32)
-        )
+        x = parts(rows[:, cols])
+        y = parts(query_buf[:, cols])
+        term = 0.0
+        for p in (2, 1, 0):
+            stacked = lax.dot_general(
+                jnp.concatenate(x[: 3 - p]), y[p], NT, preferred_element_type=jnp.float32
+            )
+            for i in reversed(range(3 - p)):
+                term = term + stacked[i * block_rows : (i + 1) * block_rows]
         total = term if total is None else total + term
     n_query_pool = query_pool.shape[0]
     n_queries = query_pick.shape[1]

time: 35.8 us -> 33.6 us (0.939)
  Pallas kernels: 34.2 us -> 32.1 us
    pallas_call x1, Pallas kernels: 34.2 us -> 32.1 us  [with_kernels(): pl.pallas_call(functools.partial(products, n_train, n_query, n_feat), out...]
where the time goes in v4:
time: 33.6 us; the launch traced here: 33.5 us
  Pallas kernels  32.1 us (96%)
  local copies, waits for them, and re-layouts  1.38 us (4%)
    pallas_call x1, Pallas kernels, with_kernels(): pl.pallas_call(functools.partial(products, n_train, n_query, n_feat), out...  32.1 us
    unnamed x1, local copies, waits for them, and re-layouts  1.38 us

profile of v4, /device:TPU:0, one launch (start us, length us, event | category | flops | bytes accessed | tf_op | source)
XLA Modules:
  0.0 33.5 jit_solution(16419204065782041040)
XLA Ops:
  0.0 32.1 %products.1 = f32[32,192]{1,0:T(8,128)} custom-call(s32[32]{0:T(128)} %train_pick_in.1, s32[1,192]{1,0:T(1,128)} %bitcast.3, f32[40,4096]{1,0:T(8,128)} %train_pool.1, f32[216,4096]{1,0:T(8,128)} %query_pool.1), custom_call_target="tpu_custom_call" | custom-call | tf_op jit(solution)/shard_map/products/pallas_call | solution.py:254
  32.1 1.4 %copy.6 = f32[192,32]{0,1:T(8,128)} copy(f32[192,32]{0,1:T(8,128)} %bitcast.2) | data formatting | bytes 49152

commit v5 on v4

--- a/solution.py
+++ b/solution.py
@@ -104,32 +104,31 @@
     ]
     for load in load_picks:
         load.start()
+    offsets = [
+        (a, b, c) for a in range(n_train) for b in range(n_query) for c in range(n_feat)
+    ][:0:-1]
+
+    def peer(a, b, c):
+        return lax.rem(t + a, n_train), lax.rem(q + b, n_query), lax.rem(f + c, n_feat)
+
+    def device(where):
+        return (g, where[0], where[1], where[2])
+
+    def place(where):
+        return (where[0] * n_query + where[1]) * n_feat + where[2]
+
+    barrier = pltpu.get_barrier_semaphore()
+    for off in offsets:
+        pl.semaphore_signal(
+            barrier, inc=1, device_id=device(peer(*off)), device_id_type=pl.DeviceIdType.MESH
+        )
+
     loads = []
     for c in range(CHUNKS):
         cols = pl.ds(c * step, step)
         load = pltpu.make_async_copy(query_pool.at[:, cols], query_buf.at[:, cols], local_sem.at[c])
         load.start()
         loads.append(load)
-
-    offsets = [
-        (a, b, c) for a in range(n_train) for b in range(n_query) for c in range(n_feat)
-    ][1:]
-
-    def peer(a, b, c):
-        return lax.rem(t + a, n_train), lax.rem(q + b, n_query), lax.rem(f + c, n_feat)
-
-    def device(where):
-        return (g, where[0], where[1], where[2])
-
-    def place(where):
-        return (where[0] * n_query + where[1]) * n_feat + where[2]
-
-    barrier = pltpu.get_barrier_semaphore()
-    for off in offsets:
-        pl.semaphore_signal(
-            barrier, inc=1, device_id=device(peer(*off)), device_id_type=pl.DeviceIdType.MESH
-        )
-
     for load in load_picks:
         load.wait()
     load_train.wait()

time: 33.6 us -> 32.3 us (0.961)
  Pallas kernels: 32.1 us -> 30.8 us
    pallas_call x1, Pallas kernels: 32.1 us -> 30.8 us  [with_kernels(): pl.pallas_call(functools.partial(products, n_train, n_query, n_feat), out...]
where the time goes in v5:
time: 32.3 us; the launch traced here: 32.2 us
  Pallas kernels  30.8 us (95%)
  local copies, waits for them, and re-layouts  1.38 us (4%)
    pallas_call x1, Pallas kernels, with_kernels(): pl.pallas_call(functools.partial(products, n_train, n_query, n_feat), out...  30.8 us
    unnamed x1, local copies, waits for them, and re-layouts  1.38 us

profile of v5, /device:TPU:0, one launch (start us, length us, event | category | flops | bytes accessed | tf_op | source)
XLA Modules:
  0.0 32.2 jit_solution(758450458516241082)
XLA Ops:
  0.0 30.8 %products.1 = f32[32,192]{1,0:T(8,128)} custom-call(s32[32]{0:T(128)} %train_pick_in.1, s32[1,192]{1,0:T(1,128)} %bitcast.3, f32[40,4096]{1,0:T(8,128)} %train_pool.1, f32[216,4096]{1,0:T(8,128)} %query_pool.1), custom_call_target="tpu_custom_call" | custom-call | tf_op jit(solution)/shard_map/products/pallas_call | solution.py:253
  30.8 1.4 %copy.6 = f32[192,32]{0,1:T(8,128)} copy(f32[192,32]{0,1:T(8,128)} %bitcast.2) | data formatting | bytes 49152

commit v6 on v5

--- a/solution.py
+++ b/solution.py
@@ -206,13 +206,6 @@
         where = peer(*off)
         rs.append(remote(part.at[slab_of(where)], terms.at[i], rs_send.at[i], rs_recv.at[i], where))
 
-    pair.wait()
-    tile[...] = mine[...] + other[...]
-    crosses[t] = tile[...]
-    tiles = []
-    for a in range(1, n_train):
-        tiles.append(remote(tile, crosses.at[t], tile_send.at[a], tile_recv.at[a], peer(a, 0, 0)))
-
     for copy in rs:
         copy.wait()
     summed = part[slab_of(here), :]
@@ -223,6 +216,13 @@
     ag = []
     for i, off in enumerate(offsets):
         ag.append(remote(slab, full.at[slab_of(here)], ag_send.at[i], ag_recv.at[i], peer(*off)))
+    pair.wait()
+    tile[...] = mine[...] + other[...]
+    crosses[t] = tile[...]
+    tiles = []
+    for a in range(1, n_train):
+        tiles.append(remote(tile, crosses.at[t], tile_send.at[a], tile_recv.at[a], peer(a, 0, 0)))
+
     for copy in ag:
         copy.wait()
     invert(full, inverse)

time: 32.3 us -> 33.7 us (1.043)
  Pallas kernels: 30.8 us -> 32.1 us
    pallas_call x1, Pallas kernels: 30.8 us -> 32.1 us  [with_kernels(): pl.pallas_call(functools.partial(products, n_train, n_query, n_feat), out...]
where the time goes in v6:
time: 33.7 us; the launch traced here: 33.5 us
  Pallas kernels  32.1 us (95%)
  local copies, waits for them, and re-layouts  1.38 us (4%)
    pallas_call x1, Pallas kernels, with_kernels(): pl.pallas_call(functools.partial(products, n_train, n_query, n_feat), out...  32.1 us
    unnamed x1, local copies, waits for them, and re-layouts  1.38 us

profile of v6, /device:TPU:0, one launch (start us, length us, event | category | flops | bytes accessed | tf_op | source)
XLA Modules:
  0.0 33.5 jit_solution(11119745841323608183)
XLA Ops:
  0.0 32.1 %products.1 = f32[32,192]{1,0:T(8,128)} custom-call(s32[32]{0:T(128)} %train_pick_in.1, s32[1,192]{1,0:T(1,128)} %bitcast.3, f32[40,4096]{1,0:T(8,128)} %train_pool.1, f32[216,4096]{1,0:T(8,128)} %query_pool.1), custom_call_target="tpu_custom_call" | custom-call | tf_op jit(solution)/shard_map/products/pallas_call | solution.py:253
  32.1 1.4 %copy.6 = f32[192,32]{0,1:T(8,128)} copy(f32[192,32]{0,1:T(8,128)} %bitcast.2) | data formatting | bytes 49152

commit v7 on v5

--- a/solution.py
+++ b/solution.py
@@ -23,11 +23,6 @@
     middle = rest.astype(jnp.bfloat16)
     low = (rest - middle.astype(jnp.float32)).astype(jnp.bfloat16)
     return high, middle, low
-
-
-def inverse_2x2(a, b, d):
-    scale = 1.0 / (a * d - b * b)
-    return d * scale, -b * scale, a * scale
 
 
 def invert(kernel_ref, inverse):
@@ -37,7 +32,7 @@
     tiles = []
     for i in range(order // 8):
         diagonal = lane == sub + 8 * i
-        tiles.append(kernel_ref[8 * i : 8 * i + 8, :] + jnp.where(diagonal, 0.5 * WIDTH, 0.0))
+        tiles.append(kernel_ref[8 * i : 8 * i + 8, :] * (1 / WIDTH) + jnp.where(diagonal, 0.5, 0.0))
 
     def columns(tile, k):
         return [jnp.broadcast_to(tile[:, k + j : k + j + 1], (8, order)) for j in range(4)]
@@ -57,14 +52,17 @@
             jnp.where(in_pivot, jnp.where(lane == k + j, 1.0, 0.0), row(tiles[home], r + j))
             for j in range(4)
         )
-        d00, d01, d11 = inverse_2x2(a00, a01, a11)
-        x00, x01 = d00 * a02 + d01 * a12, d00 * a03 + d01 * a13
-        x10, x11 = d01 * a02 + d11 * a12, d01 * a03 + d11 * a13
-        e00, e01, e11 = inverse_2x2(
-            a22 - (a02 * x00 + a12 * x10),
-            a23 - (a02 * x01 + a12 * x11),
-            a33 - (a03 * x01 + a13 * x11),
-        )
+        det = a00 * a11 - a01 * a01
+        y00, y01 = a11 * a02 - a01 * a12, a11 * a03 - a01 * a13
+        y10, y11 = a00 * a12 - a01 * a02, a00 * a13 - a01 * a03
+        s00 = det * a22 - (a02 * y00 + a12 * y10)
+        s01 = det * a23 - (a02 * y01 + a12 * y11)
+        s11 = det * a33 - (a03 * y01 + a13 * y11)
+        first = 1.0 / det
+        second = det * (1.0 / (s00 * s11 - s01 * s01))
+        d00, d01, d11 = a11 * first, -a01 * first, a00 * first
+        x00, x01, x10, x11 = y00 * first, y01 * first, y10 * first, y11 * first
+        e00, e01, e11 = s11 * second, -s01 * second, s00 * second
         v2 = r2 - (x00 * r0 + x10 * r1)
         v3 = r3 - (x01 * r0 + x11 * r1)
         w2 = e00 * v2 + e01 * v3
@@ -81,7 +79,7 @@
                     new = jnp.where(sub == r + j, w, new)
             tiles[i] = new
     for i in range(order // 8):
-        inverse[8 * i : 8 * i + 8, :] = tiles[i]
+        inverse[8 * i : 8 * i + 8, :] = tiles[i] * (1 / WIDTH)
 
 
 def products(n_train, n_query, n_feat, train_pick_in, query_pick_in, train_pool, query_pool,

time: 32.3 us -> 32.4 us (level)
  no operation moved by 1% of the time
where the time goes in v7:
time: 32.4 us; the launch traced here: 32.3 us
  Pallas kernels  30.9 us (95%)
  local copies, waits for them, and re-layouts  1.38 us (4%)
    pallas_call x1, Pallas kernels, with_kernels(): pl.pallas_call(functools.partial(products, n_train, n_query, n_feat), out...  30.9 us
    unnamed x1, local copies, waits for them, and re-layouts  1.38 us

profile of v7, /device:TPU:0, one launch (start us, length us, event | category | flops | bytes accessed | tf_op | source)
XLA Modules:
  0.0 32.3 jit_solution(16571924817142290893)
XLA Ops:
  0.0 30.9 %products.1 = f32[32,192]{1,0:T(8,128)} custom-call(s32[32]{0:T(128)} %train_pick_in.1, s32[1,192]{1,0:T(1,128)} %bitcast.3, f32[40,4096]{1,0:T(8,128)} %train_pool.1, f32[216,4096]{1,0:T(8,128)} %query_pool.1), custom_call_target="tpu_custom_call" | custom-call | tf_op jit(solution)/shard_map/products/pallas_call | solution.py:251
  30.9 1.4 %copy.6 = f32[192,32]{0,1:T(8,128)} copy(f32[192,32]{0,1:T(8,128)} %bitcast.2) | data formatting | bytes 49152

commit v8 on v7

--- a/solution.py
+++ b/solution.py
@@ -79,7 +79,7 @@
                     new = jnp.where(sub == r + j, w, new)
             tiles[i] = new
     for i in range(order // 8):
-        inverse[8 * i : 8 * i + 8, :] = tiles[i] * (1 / WIDTH)
+        inverse[8 * i : 8 * i + 8, :] = tiles[i]
 
 
 def products(n_train, n_query, n_feat, train_pick_in, query_pick_in, train_pool, query_pool,
@@ -281,7 +281,7 @@
         ),
         name="products",
     )(train_pick, query_pick.reshape(1, n_queries), train_pool, query_pool)
-    return scores.T
+    return scores.T * (1 / WIDTH)
 
 
 def with_arrays(train_pool, query_pool, train_pick, query_pick):

time: 32.4 us -> 32.4 us (level)
  other arithmetic: 0 us -> 1.38 us
  local copies, waits for them, and re-layouts: 1.38 us -> 0 us
    mul x0 -> x1, other arithmetic: none -> 1.38 us  [with_kernels(): return scores.T * (1 / WIDTH)]
    unnamed x1 -> x0, local copies, waits for them, and re-layouts: 1.38 us -> none
where the time goes in v8:
time: 32.4 us; the launch traced here: 32.3 us
  Pallas kernels  30.9 us (95%)
  other arithmetic  1.38 us (4%)
    pallas_call x1, Pallas kernels, with_kernels(): pl.pallas_call(functools.partial(products, n_train, n_query, n_feat), out...  30.9 us
    mul x1, other arithmetic, with_kernels(): return scores.T * (1 / WIDTH)  1.38 us

profile of v8, /device:TPU:0, one launch (start us, length us, event | category | flops | bytes accessed | tf_op | source)
XLA Modules:
  0.0 32.3 jit_solution(7931972052335745689)
XLA Ops:
  0.0 30.9 %products.1 = f32[32,192]{1,0:T(8,128)} custom-call(s32[32]{0:T(128)} %train_pick_in.1, s32[1,192]{1,0:T(1,128)} %bitcast.3, f32[40,4096]{1,0:T(8,128)} %train_pool.1, f32[216,4096]{1,0:T(8,128)} %query_pool.1), custom_call_target="tpu_custom_call" | custom-call | tf_op jit(solution)/shard_map/products/pallas_call | solution.py:251
  30.9 1.4 %multiply_bitcast_fusion = f32[192,32]{0,1:T(8,128)} fusion(f32[32,192]{1,0:T(8,128)} %products.1), kind=kLoop, calls=%fused_computation | loop fusion | flops 6144 | bytes 49152 | tf_op jit(solution)/shard_map/mul | solution.py:284

commit v9 on v5

--- a/solution.py
+++ b/solution.py
@@ -192,7 +192,7 @@
     pair = remote(mine, other, pair_send, pair_recv, peer(0, 0, 1))
 
     for copy in a2a:
-        copy.wait()
+        copy.wait_recv()
     gathered = blocks[...].reshape(n_train * block_rows, share)
     part[...] = dot_nt(gathered, gathered)
     slab_rows = slab.shape[0]
@@ -206,7 +206,7 @@
         where = peer(*off)
         rs.append(remote(part.at[slab_of(where)], terms.at[i], rs_send.at[i], rs_recv.at[i], where))
 
-    pair.wait()
+    pair.wait_recv()
     tile[...] = mine[...] + other[...]
     crosses[t] = tile[...]
     tiles = []
@@ -214,7 +214,7 @@
         tiles.append(remote(tile, crosses.at[t], tile_send.at[a], tile_recv.at[a], peer(a, 0, 0)))
 
     for copy in rs:
-        copy.wait()
+        copy.wait_recv()
     summed = part[slab_of(here), :]
     for i in range(len(offsets)):
         summed = summed + terms[i]
@@ -224,10 +224,10 @@
     for i, off in enumerate(offsets):
         ag.append(remote(slab, full.at[slab_of(here)], ag_send.at[i], ag_recv.at[i], peer(*off)))
     for copy in ag:
-        copy.wait()
+        copy.wait_recv()
     invert(full, inverse)
     for copy in tiles:
-        copy.wait()
+        copy.wait_recv()
     start = pl.multiple_of(t * block_rows, block_rows)
     scores_out[...] = jnp.dot(
         inverse[pl.ds(start, block_rows), :],
@@ -235,6 +235,8 @@
         precision=HIGHEST,
         preferred_element_type=jnp.float32,
     )
+    for copy in a2a + [pair] + rs + tiles + ag:
+        copy.wait_send()
 
 
 def with_kernels(sizes, train_pool, query_pool, train_pick, query_pick):

time: 32.3 us -> 32.4 us (level)
  no operation moved by 1% of the time
where the time goes in v9:
time: 32.4 us; the launch traced here: 32.2 us
  Pallas kernels  30.8 us (95%)
  local copies, waits for them, and re-layouts  1.38 us (4%)
    pallas_call x1, Pallas kernels, with_kernels(): pl.pallas_call(functools.partial(products, n_train, n_query, n_feat), out...  30.8 us
    unnamed x1, local copies, waits for them, and re-layouts  1.38 us

profile of v9, /device:TPU:0, one launch (start us, length us, event | category | flops | bytes accessed | tf_op | source)
XLA Modules:
  0.0 32.2 jit_solution(16231556562997725174)
XLA Ops:
  0.0 30.8 %products.1 = f32[32,192]{1,0:T(8,128)} custom-call(s32[32]{0:T(128)} %train_pick_in.1, s32[1,192]{1,0:T(1,128)} %bitcast.3, f32[40,4096]{1,0:T(8,128)} %train_pool.1, f32[216,4096]{1,0:T(8,128)} %query_pool.1), custom_call_target="tpu_custom_call" | custom-call | tf_op jit(solution)/shard_map/products/pallas_call | solution.py:255
  30.8 1.4 %copy.6 = f32[192,32]{0,1:T(8,128)} copy(f32[192,32]{0,1:T(8,128)} %bitcast.2) | data formatting | bytes 49152
